TPU v7x, 1024 devices: a whole 8x8x8 slice. The times are simulated.
1024 devices in a mesh: row: 64 (over y, x_hi, core), col: 16 (over x_lo, z).
Axes of the slice: x: 8 (x_hi: 4, x_lo: 2; x = x_hi * 2 + x_lo), y: 8, z: 8, core: 2. Of those that a mesh axis runs over, the one named last changes fastest.
Arguments:
- images: bfloat16 [24576, 1536], P('row'), may hold values from -8 to 8
- texts: bfloat16 [24576, 1536], P(('col', 'row')), may hold values from -8 to 8
- logit_scale: float32 [1], replicated, may hold values from 1.5 to 3
Outputs:
- loss_terms: float32 [24576], P(('row', 'col'))
- image_grad: float32 [24576, 1536], P(('row', 'col'))
All inputs are finite; a program needn't handle non-finite values.
Results may differ from a plain program's by a relative error of at most 0.0034.
Values may be sent and summed in bfloat16 or wider, within the bound.
A program may use at most 32 MiB of HBM per device.

v0:
```python
import math

import jax
import jax.numpy as jnp
from jax import lax
from jax.sharding import PartitionSpec as P


def per_device(images, texts, logit_scale):
    width = images.shape[1]
    factor = logit_scale[0] / math.sqrt(width)
    image_count = images.shape[0]
    own_rows = texts.shape[0]
    row_devices = lax.axis_size("row")
    text_count = own_rows * row_devices
    row_place = lax.axis_index("row")
    col_place = lax.axis_index("col")
    offset = row_place * image_count - col_place * text_count
    aligned = jnp.logical_and(offset >= 0, offset + image_count <= text_count)
    start_pos = jnp.clip(offset, 0, text_count - image_count)
    gathered = lax.all_gather(texts, "row", axis=0, tiled=True)
    scores = jnp.einsum("id,jd->ij", images, gathered, preferred_element_type=jnp.float32) * factor
    local_peak = jnp.max(scores, axis=1)
    diagonal_block = lax.dynamic_slice_in_dim(scores, start_pos, image_count, 1)
    positive_part = jnp.where(aligned, jnp.diagonal(diagonal_block), 0.0)
    peak_value = lax.pmax(local_peak, "col")
    partial_total = jnp.sum(jnp.exp(scores - peak_value[:, None]), axis=1)
    row_total, positive = lax.psum((partial_total, positive_part), "col")
    log_total = peak_value + jnp.log(row_total)
    paired = jnp.where(
        aligned,
        lax.dynamic_slice_in_dim(gathered, start_pos, image_count, 0).astype(jnp.float32),
        0.0,
    )
    weights = jnp.exp(scores - log_total[:, None]).astype(jnp.bfloat16)
    image_grad = lax.psum_scatter(
        jnp.dot(weights, gathered, preferred_element_type=jnp.float32) - paired,
        "col",
        scatter_dimension=0,
        tiled=True,
    )
    losses = log_total - positive
    loss_terms = lax.dynamic_slice_in_dim(losses, col_place * own_rows, own_rows, 0)
    return (loss_terms, image_grad)


def solution(mesh):
    placed = (P("row", None), P(("col", "row"), None), P())
    return jax.shard_map(
        per_device,
        mesh=mesh,
        in_specs=placed,
        out_specs=(P(("row", "col")), P(("row", "col"), None)),
        check_vma=False,
    )
```

profile of v0, /device:TPU:14, one launch (start us, length us, event | category | flops | bytes accessed | tf_op | source)
XLA Modules:
  0.0 282.3 jit_solution(81192613652499897)
XLA Ops:
  7.2 0.0 copy-start
  7.2 0.0 all-gather.2.cloned.1.call-start
  7.2 0.7 all-gather.2.cloned.1.call-update
  7.9 0.0 reduce-scatter.2.cloned.1.call-start
  8.7 107.6 %all-gather.2.cloned.1.call-done = bf16[1536,1536]{1,0:T(8,128)(2,1)} async-done(((bf16[24,1536]{1,0:T(8,128)(2,1)}), bf16[1536,1536]{1,0:T(8,128)(2,1)}) %all-gather.2.cloned.1.call-update) | async-done | bytes 4718608 | tf_op jit(solution)/shard_map/all_gather | solution.py:21
  116.2 0.0 copy-done
  116.2 4.4 %fusion.2 = (f32[384]{0:T(512)S(1)}, f32[384,1536]{1,0:T(8,128)S(1)}) fusion(f32[]{:T(128)} %bitcast, bf16[384,1536]{1,0:T(8,128)(2,1)S(1)} %copy-done, bf16[1536,1536]{1,0:T(8,128)(2,1)} %all-gather.2.cloned.1.call-done), kind=kOutput, calls=%fused_computation.11 | convolution fusion | flops 1813118592 | bytes 8259076 | tf_op jit(solution)/shard_map/id,jd->ij/dot_general | solution.py:22
  120.7 0.0 copy-start.1
  120.7 36.9 %pmax.7 = f32[384]{0:T(512)S(1)} all-reduce(f32[384]{0:T(512)S(1)} %get-tuple-element.6), channel_id=1, replica_groups=mesh['row'=64,'col'=16] {'col'}, use_global_device_ids=true, to_apply=%region_1.2 | all-reduce | flops 384 | bytes 3072 | tf_op jit(solution)/shard_map/pmax | solution.py:26
  157.6 0.0 copy-done.1
  157.6 0.5 exponential_reduce_fusion
  158.0 1.4 constant_dynamic-slice_fusion
  159.4 3.4 %gather_fusion = f32[384]{0:T(512)S(1)} fusion(f32[384,384]{1,0:T(8,128)S(1)} %constant_dynamic-slice_fusion, s32[384]{0:T(512)S(1)} %or_reduce_fusion), kind=kCustom, calls=%fused_computation | custom fusion | bytes 6144 | tf_op jit(solution)/shard_map/jit(diagonal)/cond/branch_0_fun/gather | solution.py:25
  162.9 30.6 %all-reduce = (f32[384]{0:T(512)S(1)}, f32[384]{0:T(512)S(1)}) all-reduce(f32[384]{0:T(512)S(1)} %exponential_reduce_fusion, f32[384]{0:T(512)S(1)} %broadcast_select_fusion), channel_id=1, replica_groups=mesh['row'=64,'col'=16] {'col'}, use_global_device_ids=true, to_apply=%region_3.4 | all-reduce | flops 768 | bytes 6144 | tf_op jit(solution)/shard_map/psum | solution.py:28
  193.5 6.9 %convolution_subtract_fusion = f32[384,1536]{1,0:T(8,128)} fusion(bf16[1536,1536]{1,0:T(8,128)(2,1)} %all-gather.2.cloned.1.call-done, f32[384,1536]{1,0:T(8,128)} %copy-done.1, s32[]{:T(128)S(6)} %min.4, f32[384]{0:T(512)S(1)} %get-tuple-element.5, pred[]{:T(512)S(6)} %and.5), kind=kOutput, calls=%fused_computation.2 | convolution fusion | flops 1814888448 | bytes 10618373 | tf_op jit(solution)/shard_map/dot_general | solution.py:37
  200.4 0.0 reduce-scatter.2.cloned.1.call-update
  200.4 0.6 dynamic_slice.10
  201.0 74.5 %reduce-scatter.2.cloned.1.call-done = f32[24,1536]{1,0:T(8,128)} async-done(((f32[384,1536]{1,0:T(8,128)}), f32[24,1536]{1,0:T(8,128)}) %reduce-scatter.2.cloned.1.call-update) | async-done | bytes 147472 | tf_op jit(solution)/shard_map/reduce_scatter | solution.py:36
  (3 shorter events, 0.0 us)
Async XLA Ops:
  7.2 109.1 %copy-start = (bf16[384,1536]{1,0:T(8,128)(2,1)S(1)}, bf16[384,1536]{1,0:T(8,128)(2,1)}, u32[]{:S(2)}) copy-start(bf16[384,1536]{1,0:T(8,128)(2,1)} %param.3) | copy-start | bytes 3538948
  7.2 109.1 %all-gather.2.cloned.1.call-start = ((), (), s32[]{:S(2)}) async-start(), calls=%async_computation.1 | async-start | bytes 4792320 | tf_op jit(solution)/shard_map/all_gather | solution.py:21
  7.9 267.5 %reduce-scatter.2.cloned.1.call-start = ((), (), s32[]{:S(2)}) async-start(), calls=%async_computation.2 | async-start | bytes 2506752 | tf_op jit(solution)/shard_map/reduce_scatter | solution.py:36
  120.7 36.9 %copy-start.1 = (f32[384,1536]{1,0:T(8,128)}, f32[384,1536]{1,0:T(8,128)S(1)}, u32[]{:S(2)}) copy-start(f32[384,1536]{1,0:T(8,128)S(1)} %get-tuple-element.7) | copy-start | bytes 7077892
Sparse Core Ops, SparseCore 0:
  12.5 103.6 all-gather.1
  200.5 74.8 reduce-scatter.1
where the time goes:
time: 283 us; the launch traced here: 282 us
  waiting for transfers between devices  183 us (65%)
  blocking collectives  67.5 us (24%)
  between operations  14.7 us (5%)
  matrix products  11.3 us (4%)
  local copies, waits for them, and re-layouts  5.4 us (2%)
    all_gather x1, waiting for transfers between devices, per_device(): gathered = lax.all_gather(texts, 'row', axis=0, tiled=True)  108 us
    reduce_scatter x1, waiting for transfers between devices, per_device(): lax.psum_scatter(jnp.dot(weights, gathered, preferred_element_type=jnp.fl...  74.5 us
    pmax x1, blocking collectives, per_device(): peak_value = lax.pmax(local_peak, 'col')  36.9 us
    psum x1, blocking collectives, per_device(): row_total, positive = lax.psum((partial_total, positive_part), 'col')  30.6 us
    dot_general x1, matrix products, per_device(): jnp.dot(weights, gathered, preferred_element_type=jnp.float32) - paired  6.87 us
  transfers between devices with their start and end apart: 2, of which 2 were waited for; matrix products, arithmetic and copies ran while one was open for 0% of the time, Pallas kernels for 0%

commit v1 on v0

v1 whole, which is shorter than its diff:
```python
import functools
import math

import jax
import jax.numpy as jnp
from jax import lax
from jax.experimental import pallas as pl
from jax.experimental.pallas import tpu as pltpu
from jax.sharding import PartitionSpec

MESH = pl.DeviceIdType.MESH
F32 = jnp.float32
BF16 = jnp.bfloat16
LANES = 128
WIDE = 256


def nt_dot(a, b):
    return lax.dot_general(a, b, (((1,), (1,)), ((), ())), preferred_element_type=F32)


def diagonal_mask(n, lanes):
    return lax.broadcasted_iota(jnp.int32, (n, lanes), 0) == lax.broadcasted_iota(
        jnp.int32, (n, lanes), 1
    )


def to_row(spread):
    n = spread.shape[0]
    step = min(LANES, n)
    mask = diagonal_mask(step, step)
    parts = [
        jnp.sum(jnp.where(mask, spread[i : i + step, :step], 0.0), axis=0, keepdims=True)
        for i in range(0, n, step)
    ]
    return jnp.concatenate(parts, axis=1) if len(parts) > 1 else parts[0]


def to_spread(row):
    n = row.shape[1]
    step = min(LANES, n)
    mask = diagonal_mask(step, step)
    parts = []
    for i in range(0, n, step):
        piece = jnp.broadcast_to(row[:, i : i + step], (step, step))
        column = jnp.sum(jnp.where(mask, piece, 0.0), axis=1, keepdims=True)
        parts.append(jnp.broadcast_to(column, (step, LANES)))
    return jnp.concatenate(parts, axis=0) if len(parts) > 1 else parts[0]


def kernel(
    shape,
    images_hbm,
    texts_ref,
    scale_ref,
    loss_ref,
    grad_ref,
    images,
    mine_f32,
    other_f32,
    pair_out,
    pair_in,
    paired,
    gathered,
    scores,
    weights,
    peak,
    total,
    stats,
    share_me,
    share_peer,
    logs,
    own_part,
    x_out,
    x_in,
    pair_sum,
    z_out,
    z_in,
    image_sem,
    swap_sem,
    paired_sem,
    xs,
    xr,
    ys,
    yr,
    cs,
    cr,
    ss,
    sr,
    hs,
    hr,
    zs,
    zr,
):
    n_y, n_xh, n_xl, n_z, width, own, text_step = shape
    half_width = width // 2
    rows, cols = n_y * n_xh * 2, n_xl * n_z
    block = 2 * own
    n_img = own * cols
    n_half = n_img // 2
    n_wide = width // WIDE
    r, c = lax.axis_index("row"), lax.axis_index("col")
    core = r % 2
    xh = (r // 2) % n_xh
    y = r // (2 * n_xh)
    xl = c // n_z
    z = c % n_z
    factor = scale_ref[0] * (1.0 / math.sqrt(width))
    factor2 = factor * math.log2(math.e)

    def at(y_, xh_, core_):
        return ((y_ * n_xh + xh_) * 2 + core_, c)

    other_core = at(y, xh, 1 - core)
    x_peer = [at(y, (xh + d) % n_xh, core) for d in range(n_xh)]
    y_peer = [at((y + 1) % n_y, xh, core), at((y + n_y - 1) % n_y, xh, core)]
    half_peer = (r, (1 - xl) * n_z + z)
    held_text = c * rows + r
    pair_target = (held_text // cols, held_text % cols)
    held_image = r * cols + c
    pair_source = (held_image % rows, held_image // rows)
    fixed = jnp.logical_and(pair_target[0] == r, pair_target[1] == c)

    load_images = pltpu.make_async_copy(images_hbm, images, image_sem)
    load_images.start()

    barrier = pltpu.get_barrier_semaphore()

    def greet(device):
        pl.semaphore_signal(barrier, inc=1, device_id=device, device_id_type=MESH)

    greet(other_core)
    for d in range(1, n_xh):
        greet(x_peer[d])
    for d in range(2):
        greet(y_peer[d])
    for d in range(1, cols):
        greet((r, (c + d) % cols))

    @pl.when(jnp.logical_not(fixed))
    def _():
        greet(pair_source)

    held = texts_ref[...].astype(F32)
    left, right = held[:, :half_width], held[:, half_width:]
    own_rows = pl.ds(pl.multiple_of(core * own, 8), own)
    mine_f32[own_rows, :] = jnp.where(core == 0, left, right)
    other_f32[...] = jnp.where(core == 0, right, left)
    pair_out[...] = jnp.concatenate([left, right], axis=0).astype(BF16)

    pl.semaphore_wait(barrier, cols + n_xh + 1 + jnp.where(fixed, 0, 1))

    swap = pltpu.make_async_remote_copy(
        src_ref=other_f32,
        dst_ref=mine_f32.at[own_rows, :],
        send_sem=swap_sem.at[0],
        recv_sem=swap_sem.at[1],
        device_id=other_core,
        device_id_type=MESH,
    )
    swap.start()
    pair_copy = pltpu.make_async_remote_copy(
        src_ref=pair_out,
        dst_ref=pair_in,
        send_sem=paired_sem.at[0],
        recv_sem=paired_sem.at[1],
        device_id=pair_target,
        device_id_type=MESH,
    )
    pair_local = pltpu.make_async_copy(pair_out, pair_in, paired_sem.at[2])

    last = n_y // 2

    def group(way, s):
        return 0 if s == 0 else (n_y - 1 if s == last else 2 * s - 1 + way)

    def slot(g, k):
        return gathered.at[core, pl.ds((g * n_xh + k) * block, block), :]

    def x_copy(d):
        return pltpu.make_async_remote_copy(
            src_ref=slot(0, 0),
            dst_ref=slot(0, d),
            send_sem=xs.at[d],
            recv_sem=xr.at[d],
            device_id=x_peer[d],
            device_id_type=MESH,
        )

    def y_copy(way, s, k):
        return pltpu.make_async_remote_copy(
            src_ref=slot(group(way, s), k),
            dst_ref=slot(group(way, s + 1), k),
            send_sem=ys.at[way, s, k],
            recv_sem=yr.at[way, s, k],
            device_id=y_peer[way],
            device_id_type=MESH,
        )

    def goes(way, s, k):
        return s < last - 1 or (s == last - 1 and (k < n_xh // 2) == (way == 0))

    group_rows = n_xh * block

    def core_copy(g):
        place = gathered.at[core, pl.ds(g * group_rows, group_rows), :]
        return pltpu.make_async_remote_copy(
            src_ref=place,
            dst_ref=place,
            send_sem=cs.at[g],
            recv_sem=cr.at[g],
            device_id=other_core,
            device_id_type=MESH,
        )

    def score_steps(lo, hi):
        def step(i, carry):
            part = pl.ds(pl.multiple_of(i * text_step, text_step), text_step)
            scores[:, part] = nt_dot(images[:, :half_width], gathered[0, part, :]) + nt_dot(
                images[:, half_width:], gathered[1, part, :]
            )
            return carry

        if hi > lo:
            lax.fori_loop(lo, hi, step, 0)

    swap.wait()
    gathered[core, 0:block, :] = mine_f32[...].astype(BF16)
    order = [k for k in (1, n_xh - 1) if 0 < k] + list(range(2, n_xh - 1))
    order = list(dict.fromkeys(order))
    for d in order:
        x_copy(d).start()
    for way in range(2):
        y_copy(way, 0, 0).start()
    for k in order:
        x_copy(k).wait_recv()
        for way in range(2):
            if goes(way, 0, k):
                y_copy(way, 0, k).start()
    core_copy(0).start()

    @pl.when(jnp.logical_not(fixed))
    def _():
        pair_copy.start()

    @pl.when(fixed)
    def _():
        pair_local.start()

    load_images.wait()
    done = 0
    ready = []
    for s in range(1, last + 1):
        for k in [0] + order:
            for way in range(2):
                if goes(way, s - 1, k):
                    y_copy(way, s - 1, k).wait_recv()
                    if s < last and goes(way, s, k):
                        y_copy(way, s, k).start()
        new = sorted({group(0, s), group(1, s)})
        for g in new:
            core_copy(g).start()
        for g in ([0] if s == 1 else sorted({group(0, s - 1), group(1, s - 1)})):
            core_copy(g).wait_recv()
            ready.append(g)
        upto = len(ready) * group_rows // text_step
        score_steps(done, upto)
        done = upto
    core_copy(n_y - 1).wait_recv()
    score_steps(done, rows * own // text_step)

    chunk = 64 if n_img % 64 == 0 else n_img

    def soften(i, carry):
        part = pl.ds(pl.multiple_of(i * chunk, chunk), chunk)
        value = scores[part, :]
        top = jnp.max(value, axis=1, keepdims=True)
        power = jnp.exp2((value - top) * factor2)
        weights[part, :] = power.astype(BF16)
        peak[part, :] = jnp.broadcast_to(top, (chunk, LANES))
        total[part, :] = jnp.broadcast_to(jnp.sum(power, axis=1, keepdims=True), (chunk, LANES))
        return carry

    lax.fori_loop(0, n_img // chunk, soften, 0)
    stats[c] = jnp.concatenate([to_row(peak[...]), to_row(total[...])], axis=1)

    def stat_copy(d):
        return pltpu.make_async_remote_copy(
            src_ref=stats.at[c],
            dst_ref=stats.at[c],
            send_sem=ss.at[d],
            recv_sem=sr.at[d],
            device_id=(r, (c + d) % cols),
            device_id_type=MESH,
        )

    def send_stats(d, carry):
        stat_copy(d).start()
        return carry

    lax.fori_loop(1, cols, send_stats, 0)

    def half_copy(i):
        return pltpu.make_async_remote_copy(
            src_ref=x_out.at[i],
            dst_ref=x_in.at[i],
            send_sem=hs.at[i],
            recv_sem=hr.at[i],
            device_id=half_peer,
            device_id_type=MESH,
        )

    inverse = 1.0 / total[...]
    total[...] = inverse
    per_half = half_width // WIDE

    def partial(i, carry):
        columns = pl.ds(pl.multiple_of((i % per_half) * WIDE, WIDE), WIDE)
        value = jnp.dot(
            weights[...], gathered[i // per_half, :, columns], preferred_element_type=F32
        )
        scale = total[...]
        value = value * jnp.concatenate([scale, scale], axis=1)
        low, high = value[:n_half], value[n_half:]
        x_out[i] = jnp.where(xl == 0, high, low).astype(BF16)
        half_copy(i).start()
        own_part[i] = jnp.where(xl == 0, low, high)
        return carry

    lax.fori_loop(0, n_wide, partial, 0)

    def wait_stats(d, carry):
        pltpu.make_async_remote_copy(
            src_ref=stats.at[c],
            dst_ref=stats.at[(c + cols - d) % cols],
            send_sem=ss.at[d],
            recv_sem=sr.at[d],
            device_id=(r, (c + d) % cols),
            device_id_type=MESH,
        ).wait_recv()
        return carry

    lax.fori_loop(1, cols, wait_stats, 0)
    all_peak = stats[0][:, :n_img]
    for i in range(1, cols):
        all_peak = jnp.maximum(all_peak, stats[i][:, :n_img])

    def portion(value):
        return value[:, n_img:] * jnp.exp2((value[:, :n_img] - all_peak) * factor2)

    all_total = portion(stats[0])
    for i in range(1, cols):
        all_total = all_total + portion(stats[i])
    share_me[...] = to_spread(portion(stats[c]) / all_total)
    share_peer[...] = to_spread(portion(stats[half_peer[1]]) / all_total)
    logs[...] = to_spread(all_peak * factor + jnp.log(all_total))

    half_rows = pl.ds(pl.multiple_of(xl * n_half, 8), n_half)

    def z_copy(i, d):
        return pltpu.make_async_remote_copy(
            src_ref=z_out.at[i, d],
            dst_ref=z_in.at[i, d],
            send_sem=zs.at[i, d],
            recv_sem=zr.at[i, d],
            device_id=(r, xl * n_z + (z + d) % n_z),
            device_id_type=MESH,
        )

    def join(i, carry):
        half_copy(i).wait_recv()
        me, peer = share_me[half_rows, :], share_peer[half_rows, :]
        pair_sum[i] = own_part[i] * jnp.concatenate([me, me], axis=1) + x_in[i].astype(
            F32
        ) * jnp.concatenate([peer, peer], axis=1)
        for d in range(1, n_z):
            piece = pair_sum[i, pl.ds(pl.multiple_of(((z + d) % n_z) * own, 8), own), :]
            z_out[i, d] = jnp.concatenate([piece[:, :LANES], piece[:, LANES:]], axis=0).astype(BF16)
            z_copy(i, d).start()
        return carry

    lax.fori_loop(0, n_wide, join, 0)

    @pl.when(jnp.logical_not(fixed))
    def _():
        pair_copy.wait()

    @pl.when(fixed)
    def _():
        pair_local.wait()

    folded = pair_in[...].astype(F32)
    paired[...] = jnp.concatenate([folded[:own], folded[own:]], axis=1)
    near = images[pl.ds(pl.multiple_of(16 * ((own * c) // 16), 16), own + 8), :].astype(F32)
    near = jnp.where((own * c) % 16 == 0, near[:own], near[8:])
    positive = jnp.sum(near * paired[...], axis=1, keepdims=True) * factor
    own_logs = logs[pl.ds(pl.multiple_of(c * own, 8), own), :]
    loss_ref[...] = to_row(own_logs - positive)

    def finish(i, carry):
        value = pair_sum[i, pl.ds(pl.multiple_of(z * own, 8), own), :]
        for d in range(1, n_z):
            z_copy(i, d).wait_recv()
            piece = z_in[i, d].astype(F32)
            value = value + jnp.concatenate([piece[:own], piece[own:]], axis=1)
        columns = pl.ds(pl.multiple_of(i * WIDE, WIDE), WIDE)
        grad_ref[:, columns] = value - paired[:, columns]
        return carry

    lax.fori_loop(0, n_wide, finish, 0)

    for d in order:
        x_copy(d).wait_send()
    for way in range(2):
        for s in range(last):
            for k in range(n_xh):
                if goes(way, s, k):
                    y_copy(way, s, k).wait_send()
    for g in range(n_y):
        core_copy(g).wait_send()

    def wait_stat_sends(d, carry):
        stat_copy(d).wait_send()
        return carry

    lax.fori_loop(1, cols, wait_stat_sends, 0)

    def wait_sends(i, carry):
        half_copy(i).wait_send()
        for d in range(1, n_z):
            z_copy(i, d).wait_send()
        return carry

    lax.fori_loop(0, n_wide, wait_sends, 0)


def per_device(n_xh, n_xl, text_step, images, texts, logit_scale):
    own, width = texts.shape
    rows, cols = lax.axis_size("row"), lax.axis_size("col")
    n_y = rows // (2 * n_xh)
    n_z = cols // n_xl
    n_img = images.shape[0]
    n_text = rows * own
    n_wide = width // WIDE
    shape = (n_y, n_xh, n_xl, n_z, width, own, text_step)
    dma = pltpu.SemaphoreType.DMA
    vmem = pltpu.VMEM
    loss, grad = pl.pallas_call(
        functools.partial(kernel, shape),
        out_shape=(
            jax.ShapeDtypeStruct((1, own), F32),
            jax.ShapeDtypeStruct((own, width), F32),
        ),
        in_specs=[
            pl.BlockSpec(memory_space=pl.ANY),
            pl.BlockSpec(memory_space=pltpu.VMEM),
            pl.BlockSpec(memory_space=pltpu.SMEM),
        ],
        out_specs=(
            pl.BlockSpec(memory_space=pltpu.VMEM),
            pl.BlockSpec(memory_space=pltpu.VMEM),
        ),
        scratch_shapes=[
            vmem((n_img, width), BF16),
            vmem((2 * own, width // 2), F32),
            vmem((own, width // 2), F32),
            vmem((2 * own, width // 2), BF16),
            vmem((2 * own, width // 2), BF16),
            vmem((own, width), F32),
            vmem((2, n_text, width // 2), BF16),
            vmem((n_img, n_text), F32),
            vmem((n_img, n_text), BF16),
            vmem((n_img, LANES), F32),
            vmem((n_img, LANES), F32),
            vmem((cols, 1, 2 * n_img), F32),
            vmem((n_img, LANES), F32),
            vmem((n_img, LANES), F32),
            vmem((n_img, LANES), F32),
            vmem((n_wide, n_img // 2, WIDE), F32),
            vmem((n_wide, n_img // 2, WIDE), BF16),
            vmem((n_wide, n_img // 2, WIDE), BF16),
            vmem((n_wide, n_img // 2, WIDE), F32),
            vmem((n_wide, n_z, 2 * own, WIDE // 2), BF16),
            vmem((n_wide, n_z, 2 * own, WIDE // 2), BF16),
            dma(()),
            dma((2,)),
            dma((3,)),
            dma((n_xh,)),
            dma((n_xh,)),
            dma((2, n_y // 2, n_xh)),
            dma((2, n_y // 2, n_xh)),
            dma((n_y,)),
            dma((n_y,)),
            dma((cols,)),
            dma((cols,)),
            dma((n_wide,)),
            dma((n_wide,)),
            dma((n_wide, n_z)),
            dma((n_wide, n_z)),
        ],
        compiler_params=pltpu.CompilerParams(
            collective_id=0, has_side_effects=True, vmem_limit_bytes=40 * 1024 * 1024
        ),
        cost_estimate=pl.CostEstimate(
            flops=4 * n_img * n_text * width,
            bytes_accessed=2 * n_img * width,
            transcendentals=n_img * n_text,
        ),
    )(images, texts, logit_scale)
    return loss.reshape(own), grad


def solution(mesh, n_xh=4, n_xl=2, text_step=256):
    placed = (
        PartitionSpec("row", None),
        PartitionSpec(("col", "row"), None),
        PartitionSpec(),
    )
    return jax.shard_map(
        functools.partial(per_device, n_xh, n_xl, text_step),
        mesh=mesh,
        in_specs=placed,
        out_specs=(PartitionSpec(("row", "col")), PartitionSpec(("row", "col"), None)),
        check_vma=False,
    )
```

time: 283 us -> 97.5 us (0.34)
  the two profiles are of different devices: /device:TPU:14 before, /device:TPU:1 now
where the time goes in v1:
time: 97.5 us; the launch traced here: 96.1 us
  Pallas kernels  91.5 us (94%)
  local copies, waits for them, and re-layouts  3.32 us (3%)
  between operations  1.29 us (1%)
    pallas_call x1, Pallas kernels, per_device(): pl.pallas_call(functools.partial(kernel, shape), out_shape=(jax.ShapeDtyp...  91.5 us
    unnamed x6, local copies, waits for them, and re-layouts  3.32 us

profile of v1, /device:TPU:1, one launch (start us, length us, event | category | flops | bytes accessed | tf_op | source)
XLA Modules:
  0.0 96.1 jit_solution(8237309216734082122)
XLA Ops:
  1.3 0.0 copy-start
  1.3 1.3 %copy-done = bf16[384,1536]{1,0:T(8,128)(2,1)S(1)} copy-done((bf16[384,1536]{1,0:T(8,128)(2,1)S(1)}, bf16[384,1536]{1,0:T(8,128)(2,1)}, u32[]{:S(2)}) %copy-start) | copy-done | bytes 1179672
  2.5 0.0 copy-start.1
  2.5 0.9 copy-done.1
  3.4 91.5 %shard_map.50 = (f32[1,24]{1,0:T(1,128)S(1)}, f32[24,1536]{1,0:T(8,128)S(1)}) custom-call(bf16[384,1536]{1,0:T(8,128)(2,1)S(1)} %copy-done, bf16[24,1536]{1,0:T(8,128)(2,1)S(1)} %copy-done.1, f32[1]{0:T(128)S(6)} %copy.7.scale_ref), custom_call_target="tpu_custom_call" | custom-call | flops 3623878656 | bytes 1179648 | tf_op jit(solution)/shard_map/pallas_call | solution.py:448
  94.9 0.5 copy.8
  95.4 0.7 copy.9
Async XLA Ops:
  1.3 1.3 %copy-start = (bf16[384,1536]{1,0:T(8,128)(2,1)S(1)}, bf16[384,1536]{1,0:T(8,128)(2,1)}, u32[]{:S(2)}) copy-start(bf16[384,1536]{1,0:T(8,128)(2,1)} %images_hbm.1) | copy-start | bytes 3538948
  2.5 0.9 copy-start.1

commit v2 on v1

--- a/solution.py
+++ b/solution.py
@@ -1,4 +1,5 @@
 import functools
+import heapq
 import math
 
 import jax
@@ -48,19 +49,82 @@
     return jnp.concatenate(parts, axis=0) if len(parts) > 1 else parts[0]
 
 
+def arrivals(n_y, block_us):
+    last = n_y // 2
+    free = {}
+    sent = {}
+    queue = []
+
+    def send(now, piece):
+        kind = piece[0]
+        if kind == "x":
+            link = ("x", piece[2] % 2)
+            cost = (2 / 3 if piece[1] == 0 else 1 / 3) * (2 if piece[2] < 2 else 1)
+        elif kind == "a":
+            link, cost = ("y", piece[1]), 2 / 3
+        else:
+            link, cost = ("y", piece[1]), (1 / 3 if piece[2] < last - 1 else 1 / 6)
+        begin = max(now, free.get(link, 0.0))
+        free[link] = begin + cost * block_us
+        heapq.heappush(queue, (free[link] + 2.0, len(sent), piece))
+        sent[piece] = now
+
+    def both(kind, *rest):
+        return [(kind, way) + rest for way in range(2)]
+
+    start = [("x", 0, 0), ("x", 0, 1)] + both("b", 0) + both("a", 0, 0) + [("x", 1, 0), ("x", 1, 1)]
+    for piece in start:
+        send(0.0, piece)
+    got, result = set(), []
+    while queue:
+        now, _, piece = heapq.heappop(queue)
+        got.add(piece)
+        then = []
+        if piece[0] == "x":
+            _, j, i = piece
+            if i < 2:
+                then.append(("x", j, i + 2))
+                if j == 0:
+                    then += [p for p in both("a", 0, 1 if i == 0 else 3) if a_goes(last, *p[1:])]
+            elif j == 0 and ("x", 0, 5 - i) in got:
+                then += [p for p in both("a", 0, 2) if a_goes(last, *p[1:])]
+        elif piece[0] == "a":
+            _, way, s, k = piece
+            if s + 1 < last and a_goes(last, way, s + 1, k):
+                then.append(("a", way, s + 1, k))
+        else:
+            _, way, s = piece
+            if s + 1 < last:
+                then.append(("b", way, s + 1))
+            if s + 1 < last or ("b", 1 - way, s) in got:
+                g = group_of(n_y, way, s + 1)
+                then += [("x", 1 + g, 0), ("x", 1 + g, 1)]
+        for p in then:
+            send(now, p)
+        result.append((now, piece, then))
+    return start, result
+
+
+def a_goes(last, way, s, k):
+    return s < last - 1 or (k < 2) == (way == 0)
+
+
+def group_of(n_y, way, s):
+    return 0 if s == 0 else (n_y - 1 if s == n_y // 2 else 2 * s - 1 + way)
+
+
 def kernel(
     shape,
     images_hbm,
-    texts_ref,
+    texts_hbm,
     scale_ref,
     loss_ref,
     grad_ref,
     images,
-    mine_f32,
-    other_f32,
-    pair_out,
+    texts,
     pair_in,
     paired,
+    folded,
     gathered,
     scores,
     weights,
@@ -76,13 +140,14 @@
     pair_sum,
     z_out,
     z_in,
-    image_sem,
-    swap_sem,
+    load_sem,
     paired_sem,
     xs,
     xr,
-    ys,
-    yr,
+    as_,
+    ar,
+    bs,
+    br,
     cs,
     cr,
     ss,
@@ -96,9 +161,11 @@
     half_width = width // 2
     rows, cols = n_y * n_xh * 2, n_xl * n_z
     block = 2 * own
+    cut = block * 2 // 3
     n_img = own * cols
     n_half = n_img // 2
     n_wide = width // WIDE
+    last = n_y // 2
     r, c = lax.axis_index("row"), lax.axis_index("col")
     core = r % 2
     xh = (r // 2) % n_xh
@@ -112,108 +179,130 @@
         return ((y_ * n_xh + xh_) * 2 + core_, c)
 
     other_core = at(y, xh, 1 - core)
-    x_peer = [at(y, (xh + d) % n_xh, core) for d in range(n_xh)]
+    x_peer = [at(y, (xh + 1) % n_xh, core), at(y, (xh + n_xh - 1) % n_xh, core)]
     y_peer = [at((y + 1) % n_y, xh, core), at((y + n_y - 1) % n_y, xh, core)]
     half_peer = (r, (1 - xl) * n_z + z)
+
     held_text = c * rows + r
     pair_target = (held_text // cols, held_text % cols)
     held_image = r * cols + c
     pair_source = (held_image % rows, held_image // rows)
     fixed = jnp.logical_and(pair_target[0] == r, pair_target[1] == c)
 
-    load_images = pltpu.make_async_copy(images_hbm, images, image_sem)
+    load_texts = pltpu.make_async_copy(texts_hbm, texts, load_sem.at[0])
+    load_texts.start()
+    load_images = pltpu.make_async_copy(images_hbm, images, load_sem.at[1])
     load_images.start()
 
     barrier = pltpu.get_barrier_semaphore()
 
     def greet(device):
         pl.semaphore_signal(barrier, inc=1, device_id=device, device_id_type=MESH)
-
-    greet(other_core)
-    for d in range(1, n_xh):
-        greet(x_peer[d])
-    for d in range(2):
-        greet(y_peer[d])
-    for d in range(1, cols):
-        greet((r, (c + d) % cols))
 
     @pl.when(jnp.logical_not(fixed))
     def _():
         greet(pair_source)
 
-    held = texts_ref[...].astype(F32)
-    left, right = held[:, :half_width], held[:, half_width:]
-    own_rows = pl.ds(pl.multiple_of(core * own, 8), own)
-    mine_f32[own_rows, :] = jnp.where(core == 0, left, right)
-    other_f32[...] = jnp.where(core == 0, right, left)
-    pair_out[...] = jnp.concatenate([left, right], axis=0).astype(BF16)
-
-    pl.semaphore_wait(barrier, cols + n_xh + 1 + jnp.where(fixed, 0, 1))
-
-    swap = pltpu.make_async_remote_copy(
-        src_ref=other_f32,
-        dst_ref=mine_f32.at[own_rows, :],
-        send_sem=swap_sem.at[0],
-        recv_sem=swap_sem.at[1],
-        device_id=other_core,
-        device_id_type=MESH,
-    )
-    swap.start()
-    pair_copy = pltpu.make_async_remote_copy(
-        src_ref=pair_out,
-        dst_ref=pair_in,
-        send_sem=paired_sem.at[0],
-        recv_sem=paired_sem.at[1],
-        device_id=pair_target,
-        device_id_type=MESH,
-    )
-    pair_local = pltpu.make_async_copy(pair_out, pair_in, paired_sem.at[2])
-
-    last = n_y // 2
-
-    def group(way, s):
-        return 0 if s == 0 else (n_y - 1 if s == last else 2 * s - 1 + way)
-
-    def slot(g, k):
-        return gathered.at[core, pl.ds((g * n_xh + k) * block, block), :]
-
-    def x_copy(d):
+    def greet_column(d, carry):
+        greet((r, (c + d) % cols))
+        return carry
+
+    lax.fori_loop(1, cols, greet_column, 0)
+    for peer in x_peer + y_peer + [other_core]:
+        greet(peer)
+
+    load_texts.wait()
+    held = texts[...].astype(F32)
+    folded[core, 0:block, :] = jnp.concatenate(
+        [held[:, :half_width], held[:, half_width:]], axis=0
+    ).astype(BF16)
+    pl.semaphore_wait(barrier, cols + 4 + jnp.where(fixed, 0, 1))
+
+    def piece_at(g, k, first, columns=None):
+        begin = (g * n_xh + k) * block
+        part = pl.ds(begin, cut) if first else pl.ds(begin + cut, block - cut)
+        if columns is None:
+            return folded.at[core, part, :]
+        return folded.at[core, part, pl.ds(columns * (half_width // 2), half_width // 2)]
+
+    def push(src, dst, send_sem, recv_sem, device):
         return pltpu.make_async_remote_copy(
-            src_ref=slot(0, 0),
-            dst_ref=slot(0, d),
-            send_sem=xs.at[d],
-            recv_sem=xr.at[d],
-            device_id=x_peer[d],
+            src_ref=src,
+            dst_ref=dst,
+            send_sem=send_sem,
+            recv_sem=recv_sem,
+            device_id=device,
             device_id_type=MESH,
         )
 
-    def y_copy(way, s, k):
-        return pltpu.make_async_remote_copy(
-            src_ref=slot(group(way, s), k),
-            dst_ref=slot(group(way, s + 1), k),
-            send_sem=ys.at[way, s, k],
-            recv_sem=yr.at[way, s, k],
-            device_id=y_peer[way],
-            device_id_type=MESH,
+    def copy_of(piece):
+        if piece[0] == "x":
+            _, j, i = piece
+            g, first = max(j - 1, 0), j == 0
+            columns = None if i < 2 else i - 2
+            here = 0 if i < 2 else (1 if i == 2 else 3)
+            there = (1, 3, 2, 2)[i]
+            return push(
+                piece_at(g, here, first, columns),
+                piece_at(g, there, first, columns),
+                xs.at[j, i],
+                xr.at[j, i],
+                x_peer[i % 2],
+            )
+        if piece[0] == "a":
+            _, way, s, k = piece
+            return push(
+                piece_at(group_of(n_y, way, s), k, True),
+                piece_at(group_of(n_y, way, s + 1), k, True),
+                as_.at[way, s, k],
+                ar.at[way, s, k],
+                y_peer[way],
+            )
+        _, way, s = piece
+        columns = None if s < last - 1 else way
+        return push(
+            piece_at(group_of(n_y, way, s), 0, False, columns),
+            piece_at(group_of(n_y, way, s + 1), 0, False, columns),
+            bs.at[way, s],
+            br.at[way, s],
+            y_peer[way],
         )
 
-    def goes(way, s, k):
-        return s < last - 1 or (s == last - 1 and (k < n_xh // 2) == (way == 0))
-
     group_rows = n_xh * block
 
     def core_copy(g):
-        place = gathered.at[core, pl.ds(g * group_rows, group_rows), :]
-        return pltpu.make_async_remote_copy(
-            src_ref=place,
-            dst_ref=place,
-            send_sem=cs.at[g],
-            recv_sem=cr.at[g],
-            device_id=other_core,
-            device_id_type=MESH,
+        place = folded.at[core, pl.ds(g * group_rows, group_rows), :]
+        return push(place, place, cs.at[g], cr.at[g], other_core)
+
+    def pair_copy():
+        return push(
+            folded.at[core, 0:block, :], pair_in, paired_sem.at[0], paired_sem.at[1], pair_target
         )
 
-    def score_steps(lo, hi):
+    def pair_local():
+        return pltpu.make_async_copy(folded.at[core, 0:block, :], pair_in, paired_sem.at[0])
+
+    def send_paired():
+        @pl.when(jnp.logical_not(fixed))
+        def _():
+            pair_copy().start()
+
+        @pl.when(fixed)
+        def _():
+            pair_local().start()
+
+    def unfold(g):
+        def one(k, carry):
+            begin = pl.multiple_of((g * n_xh + k) * block, block)
+            part = pl.ds(begin, block)
+            one_, two = folded[0, part, :].astype(F32), folded[1, part, :].astype(F32)
+            gathered[0, part, :] = jnp.concatenate([one_[:own], two[:own]], axis=0).astype(BF16)
+            gathered[1, part, :] = jnp.concatenate([one_[own:], two[own:]], axis=0).astype(BF16)
+            return carry
+
+        lax.fori_loop(0, n_xh, one, 0)
+
+    def score(lo, hi):
         def step(i, carry):
             part = pl.ds(pl.multiple_of(i * text_step, text_step), text_step)
             scores[:, part] = nt_dot(images[:, :half_width], gathered[0, part, :]) + nt_dot(
@@ -221,53 +310,53 @@
             )
             return carry
 
-        if hi > lo:
-            lax.fori_loop(lo, hi, step, 0)
-
-    swap.wait()
-    gathered[core, 0:block, :] = mine_f32[...].astype(BF16)
-    order = [k for k in (1, n_xh - 1) if 0 < k] + list(range(2, n_xh - 1))
-    order = list(dict.fromkeys(order))
-    for d in order:
-        x_copy(d).start()
-    for way in range(2):
-        y_copy(way, 0, 0).start()
-    for k in order:
-        x_copy(k).wait_recv()
-        for way in range(2):
-            if goes(way, 0, k):
-                y_copy(way, 0, k).start()
-    core_copy(0).start()
-
-    @pl.when(jnp.logical_not(fixed))
-    def _():
-        pair_copy.start()
-
-    @pl.when(fixed)
-    def _():
-        pair_local.start()
-
+        lax.fori_loop(lo, hi, step, 0)
+
+    start, order = arrivals(n_y, 1.6)
+    for piece in start:
+        copy_of(piece).start()
+
+    missing = {g: {("x", 1 + g, i) for i in range(4)} for g in range(n_y)}
+    missing[0] |= {("x", 0, i) for i in range(4)}
+    for _, piece, _ in order:
+        if piece[0] == "a":
+            missing[group_of(n_y, piece[1], piece[2] + 1)].add(piece)
+        elif piece[0] == "b":
+            missing[group_of(n_y, piece[1], piece[2] + 1)].add(piece)
     load_images.wait()
-    done = 0
-    ready = []
-    for s in range(1, last + 1):
-        for k in [0] + order:
-            for way in range(2):
-                if goes(way, s - 1, k):
-                    y_copy(way, s - 1, k).wait_recv()
-                    if s < last and goes(way, s, k):
-                        y_copy(way, s, k).start()
-        new = sorted({group(0, s), group(1, s)})
-        for g in new:
-            core_copy(g).start()
-        for g in ([0] if s == 1 else sorted({group(0, s - 1), group(1, s - 1)})):
+    flying, ready, done = [], set(), 0
+
+    def land(now):
+        nonlocal done
+        while flying and flying[0][0] <= now:
+            g = flying.pop(0)[1]
             core_copy(g).wait_recv()
-            ready.append(g)
-        upto = len(ready) * group_rows // text_step
-        score_steps(done, upto)
-        done = upto
-    core_copy(n_y - 1).wait_recv()
-    score_steps(done, rows * own // text_step)
+            unfold(g)
+            ready.add(g)
+            upto = done
+            while (upto + 1) * text_step <= n_y * n_xh * block and all(
+                g_ in ready
+                for g_ in range(
+                    upto * text_step // group_rows, ((upto + 1) * text_step - 1) // group_rows + 1
+                )
+            ):
+                upto += 1
+            if upto > done:
+                score(done, upto)
+                done = upto
+
+    for now, piece, then in order:
+        land(now)
+        copy_of(piece).wait_recv()
+        for p in then:
+            copy_of(p).start()
+        for g in range(n_y):
+            if piece in missing[g]:
+                missing[g].remove(piece)
+                if not missing[g]:
+                    core_copy(g).start()
+                    flying.append((now + 3.0, g))
+    land(1e9)
 
     chunk = 64 if n_img % 64 == 0 else n_img
 
@@ -328,6 +417,7 @@
         return carry
 
     lax.fori_loop(0, n_wide, partial, 0)
+    send_paired()
 
     def wait_stats(d, carry):
         pltpu.make_async_remote_copy(
@@ -383,14 +473,14 @@
 
     @pl.when(jnp.logical_not(fixed))
     def _():
-        pair_copy.wait()
+        pair_copy().wait()
 
     @pl.when(fixed)
     def _():
-        pair_local.wait()
-
-    folded = pair_in[...].astype(F32)
-    paired[...] = jnp.concatenate([folded[:own], folded[own:]], axis=1)
+        pair_local().wait()
+
+    block_in = pair_in[...].astype(F32)
+    paired[...] = jnp.concatenate([block_in[:own], block_in[own:]], axis=1)
     near = images[pl.ds(pl.multiple_of(16 * ((own * c) // 16), 16), own + 8), :].astype(F32)
     near = jnp.where((own * c) % 16 == 0, near[:own], near[8:])
     positive = jnp.sum(near * paired[...], axis=1, keepdims=True) * factor
@@ -409,13 +499,11 @@
 
     lax.fori_loop(0, n_wide, finish, 0)
 
-    for d in order:
-        x_copy(d).wait_send()
-    for way in range(2):
-        for s in range(last):
-            for k in range(n_xh):
-                if goes(way, s, k):
-                    y_copy(way, s, k).wait_send()
+    for piece in start:
+        copy_of(piece).wait_send()
+    for _, _, then in order:
+        for piece in then:
+            copy_of(piece).wait_send()
     for g in range(n_y):
         core_copy(g).wait_send()
 
@@ -453,7 +541,7 @@
         ),
         in_specs=[
             pl.BlockSpec(memory_space=pl.ANY),
-            pl.BlockSpec(memory_space=pltpu.VMEM),
+            pl.BlockSpec(memory_space=pl.ANY),
             pl.BlockSpec(memory_space=pltpu.SMEM),
         ],
         out_specs=(
@@ -462,11 +550,10 @@
         ),
         scratch_shapes=[
             vmem((n_img, width), BF16),
-            vmem((2 * own, width // 2), F32),
-            vmem((own, width // 2), F32),
-            vmem((2 * own, width // 2), BF16),
+            vmem((own, width), BF16),
             vmem((2 * own, width // 2), BF16),
             vmem((own, width), F32),
+            vmem((2, n_text, width // 2), BF16),
             vmem((2, n_text, width // 2), BF16),
             vmem((n_img, n_text), F32),
             vmem((n_img, n_text), BF16),
@@ -482,13 +569,14 @@
             vmem((n_wide, n_img // 2, WIDE), F32),
             vmem((n_wide, n_z, 2 * own, WIDE // 2), BF16),
             vmem((n_wide, n_z, 2 * own, WIDE // 2), BF16),
-            dma(()),
             dma((2,)),
-            dma((3,)),
-            dma((n_xh,)),
-            dma((n_xh,)),
+            dma((2,)),
+            dma((1 + n_y, 4)),
+            dma((1 + n_y, 4)),
             dma((2, n_y // 2, n_xh)),
             dma((2, n_y // 2, n_xh)),
+            dma((2, n_y // 2)),
+            dma((2, n_y // 2)),
             dma((n_y,)),
             dma((n_y,)),
             dma((cols,)),
@@ -499,7 +587,7 @@
             dma((n_wide, n_z)),
         ],
         compiler_params=pltpu.CompilerParams(
-            collective_id=0, has_side_effects=True, vmem_limit_bytes=40 * 1024 * 1024
+            collective_id=0, has_side_effects=True, vmem_limit_bytes=60 * 1024 * 1024
         ),
         cost_estimate=pl.CostEstimate(
             flops=4 * n_img * n_text * width,

time: 97.5 us -> 86.9 us (0.89)
  the two profiles are of different devices: /device:TPU:1 before, /device:TPU:32 now
where the time goes in v2:
time: 86.9 us; the launch traced here: 86.7 us
  Pallas kernels  82.7 us (95%)
  local copies, waits for them, and re-layouts  2.74 us (3%)
  between operations  1.28 us (1%)
    pallas_call x1, Pallas kernels, per_device(): pl.pallas_call(functools.partial(kernel, shape), out_shape=(jax.ShapeDtyp...  82.7 us
    unnamed x2, local copies, waits for them, and re-layouts  2.74 us

profile of v2, /device:TPU:32, one launch (start us, length us, event | category | flops | bytes accessed | tf_op | source)
XLA Modules:
  0.0 86.7 jit_solution(8794165278892431493)
XLA Ops:
  1.3 82.7 %shard_map.50 = (f32[1,24]{1,0:T(1,128)}, f32[24,1536]{1,0:T(8,128)}) custom-call(bf16[384,1536]{1,0:T(8,128)(2,1)} %images_hbm.1, bf16[24,1536]{1,0:T(8,128)(2,1)} %texts_hbm.1, f32[1]{0:T(128)S(6)} %copy.7.scale_ref), custom_call_target="tpu_custom_call" | custom-call | flops 3623878656 | bytes 1179648 | tf_op jit(solution)/shard_map/pallas_call | solution.py:536
  84.0 1.2 %copy.8 = f32[24]{0:T(128)} copy(f32[24]{0:T(128)} %bitcast.1) | data formatting | bytes 192
  85.1 1.6 %copy.9 = f32[24,1536]{1,0:T(8,128)} copy(f32[24,1536]{1,0:T(8,128)} %get-tuple-element.9) | data formatting | bytes 294912

commit v3 on v2

--- a/solution.py
+++ b/solution.py
@@ -49,64 +49,79 @@
     return jnp.concatenate(parts, axis=0) if len(parts) > 1 else parts[0]
 
 
-def arrivals(n_y, block_us):
+def origin(last, piece):
+    if piece[0] == "b":
+        return (0, piece[2] + 1) if piece[2] + 1 < last else (last - 1, 1)
+    d = piece[2] + 1
+    if piece[3] == 2 and d > 1:
+        return (0, 2) if d == 2 else (2, d - 2)
+    return (d - 1, 1)
+
+
+def a_goes(last, way, s, k):
+    return s < last - 1 or (k % 2 == 0) == (way == 0)
+
+
+def arrivals(n_y, block_us, latency):
     last = n_y // 2
     free = {}
-    sent = {}
     queue = []
 
+    def along_y(kind, way, d, *k):
+        pieces = [(kind, way, s) + k for s in range(last)]
+        return [
+            p
+            for p in pieces
+            if origin(last, p)[0] == d and (kind == "b" or a_goes(last, *p[1:]))
+        ]
+
+    def both(kind, d, *k):
+        return along_y(kind, 0, d, *k) + along_y(kind, 1, d, *k)
+
     def send(now, piece):
-        kind = piece[0]
-        if kind == "x":
+        if piece[0] == "x":
             link = ("x", piece[2] % 2)
+            hops = 2
             cost = (2 / 3 if piece[1] == 0 else 1 / 3) * (2 if piece[2] < 2 else 1)
-        elif kind == "a":
-            link, cost = ("y", piece[1]), 2 / 3
         else:
-            link, cost = ("y", piece[1]), (1 / 3 if piece[2] < last - 1 else 1 / 6)
-        begin = max(now, free.get(link, 0.0))
-        free[link] = begin + cost * block_us
-        heapq.heappush(queue, (free[link] + 2.0, len(sent), piece))
-        sent[piece] = now
-
-    def both(kind, *rest):
-        return [(kind, way) + rest for way in range(2)]
-
-    start = [("x", 0, 0), ("x", 0, 1)] + both("b", 0) + both("a", 0, 0) + [("x", 1, 0), ("x", 1, 1)]
+            link = ("y", piece[1])
+            hops = origin(last, piece)[1]
+            cost = hops * (2 / 3 if piece[0] == "a" else (1 / 3 if piece[2] < last - 1 else 1 / 6))
+        free[link] = max(now, free.get(link, 0.0)) + cost * block_us
+        heapq.heappush(queue, (free[link] + latency + 0.3 * (hops - 1), len(sent), piece))
+        sent.append(piece)
+
+    sent = []
+    start = [("x", 0, 0), ("x", 0, 1)] + both("a", 0, 0) + both("b", 0) + [("x", 1, 0), ("x", 1, 1)]
     for piece in start:
         send(0.0, piece)
-    got, result = set(), []
+    got, result, clock = set(), [], 0.0
     while queue:
         now, _, piece = heapq.heappop(queue)
+        clock = max(now, clock + 0.05)
         got.add(piece)
         then = []
         if piece[0] == "x":
             _, j, i = piece
             if i < 2:
+                if j == 0:
+                    then += both("a", 0, 1 if i == 0 else 3)
                 then.append(("x", j, i + 2))
-                if j == 0:
-                    then += [p for p in both("a", 0, 1 if i == 0 else 3) if a_goes(last, *p[1:])]
             elif j == 0 and ("x", 0, 5 - i) in got:
-                then += [p for p in both("a", 0, 2) if a_goes(last, *p[1:])]
+                then += both("a", 0, 2)
         elif piece[0] == "a":
             _, way, s, k = piece
-            if s + 1 < last and a_goes(last, way, s + 1, k):
-                then.append(("a", way, s + 1, k))
+            then += along_y("a", way, s + 1, k)
         else:
             _, way, s = piece
-            if s + 1 < last:
-                then.append(("b", way, s + 1))
+            then += along_y("b", way, s + 1)
             if s + 1 < last or ("b", 1 - way, s) in got:
                 g = group_of(n_y, way, s + 1)
                 then += [("x", 1 + g, 0), ("x", 1 + g, 1)]
         for p in then:
-            send(now, p)
-        result.append((now, piece, then))
+            send(clock, p)
+        result.append((clock, piece, then))
     return start, result
-
-
-def a_goes(last, way, s, k):
-    return s < last - 1 or (k < 2) == (way == 0)
 
 
 def group_of(n_y, way, s):
@@ -123,6 +138,7 @@
     images,
     texts,
     pair_in,
+    relay,
     paired,
     folded,
     gathered,
@@ -142,6 +158,7 @@
     z_in,
     load_sem,
     paired_sem,
+    ps,
     xs,
     xr,
     as_,
@@ -180,14 +197,19 @@
 
     other_core = at(y, xh, 1 - core)
     x_peer = [at(y, (xh + 1) % n_xh, core), at(y, (xh + n_xh - 1) % n_xh, core)]
-    y_peer = [at((y + 1) % n_y, xh, core), at((y + n_y - 1) % n_y, xh, core)]
+
+    def y_peer(way, hops):
+        return at((y + (hops if way == 0 else n_y - hops)) % n_y, xh, core)
+
     half_peer = (r, (1 - xl) * n_z + z)
 
-    held_text = c * rows + r
-    pair_target = (held_text // cols, held_text % cols)
     held_image = r * cols + c
-    pair_source = (held_image % rows, held_image // rows)
-    fixed = jnp.logical_and(pair_target[0] == r, pair_target[1] == c)
+    pair_col = ((r // 2) * 2 * cols) // rows
+    pair_source = ((r // 2) * 2 + (held_image % rows) % 2, pair_col)
+    near_side = pair_col // n_z == xl
+    aligned = pair_col == c
+    fixed = jnp.logical_and(pair_source[0] == r, aligned)
+    near_other = jnp.logical_and(near_side, jnp.logical_not(fixed))
 
     load_texts = pltpu.make_async_copy(texts_hbm, texts, load_sem.at[0])
     load_texts.start()
@@ -199,7 +221,7 @@
     def greet(device):
         pl.semaphore_signal(barrier, inc=1, device_id=device, device_id_type=MESH)
 
-    @pl.when(jnp.logical_not(fixed))
+    @pl.when(near_other)
     def _():
         greet(pair_source)
 
@@ -208,7 +230,7 @@
         return carry
 
     lax.fori_loop(1, cols, greet_column, 0)
-    for peer in x_peer + y_peer + [other_core]:
+    for peer in [y_peer(0, hops) for hops in range(1, n_y)] + x_peer + [other_core]:
         greet(peer)
 
     load_texts.wait()
@@ -216,7 +238,7 @@
     folded[core, 0:block, :] = jnp.concatenate(
         [held[:, :half_width], held[:, half_width:]], axis=0
     ).astype(BF16)
-    pl.semaphore_wait(barrier, cols + 4 + jnp.where(fixed, 0, 1))
+    pl.semaphore_wait(barrier, cols + n_y + 1 + jnp.where(aligned, n_z, 0) - jnp.where(fixed, 1, 0))
 
     def piece_at(g, k, first, columns=None):
         begin = (g * n_xh + k) * block
@@ -252,20 +274,20 @@
         if piece[0] == "a":
             _, way, s, k = piece
             return push(
-                piece_at(group_of(n_y, way, s), k, True),
+                piece_at(group_of(n_y, way, origin(last, piece)[0]), k, True),
                 piece_at(group_of(n_y, way, s + 1), k, True),
                 as_.at[way, s, k],
                 ar.at[way, s, k],
-                y_peer[way],
+                y_peer(way, origin(last, piece)[1]),
             )
         _, way, s = piece
         columns = None if s < last - 1 else way
         return push(
-            piece_at(group_of(n_y, way, s), 0, False, columns),
+            piece_at(group_of(n_y, way, origin(last, piece)[0]), 0, False, columns),
             piece_at(group_of(n_y, way, s + 1), 0, False, columns),
             bs.at[way, s],
             br.at[way, s],
-            y_peer[way],
+            y_peer(way, origin(last, piece)[1]),
         )
 
     group_rows = n_xh * block
@@ -274,22 +296,51 @@
         place = folded.at[core, pl.ds(g * group_rows, group_rows), :]
         return push(place, place, cs.at[g], cr.at[g], other_core)
 
-    def pair_copy():
-        return push(
-            folded.at[core, 0:block, :], pair_in, paired_sem.at[0], paired_sem.at[1], pair_target
+    def pair_copies(g, act):
+        step = (g + 1) // 2
+        y_from = (y + (n_y - step if g % 2 == 1 else step)) % n_y
+
+        def one(k, carry):
+            text = c * rows + (y_from * n_xh + (xh + n_xh - k) % n_xh) * 2 + core
+            to_r, to_c = text // cols, text % cols
+            here = jnp.logical_and(to_r == r, to_c % n_z == z)
+            leaves = jnp.logical_and(to_r // 2 == r // 2, jnp.logical_not(here))
+            place = folded.at[core, pl.ds(pl.multiple_of((g * n_xh + k) * block, block), block), :]
+            target = (to_r, xl * n_z + to_c % n_z)
+
+            @pl.when(jnp.logical_and(leaves, to_c // n_z == xl))
+            def _():
+                act(push(place, pair_in, ps.at[g, k], paired_sem.at[0], target))
+
+            @pl.when(jnp.logical_and(leaves, to_c // n_z != xl))
+            def _():
+                act(push(place, relay, ps.at[g, k], paired_sem.at[1], target))
+
+            return carry
+
+        lax.fori_loop(0, n_xh, one, 0)
+
+    def held_place(image):
+        text = image % rows
+        away = (y + n_y - text // (2 * n_xh)) % n_y
+        g = jnp.where(
+            away == last, n_y - 1, jnp.where(away > last, 2 * (n_y - away), jnp.maximum(2 * away - 1, 0))
         )
-
-    def pair_local():
-        return pltpu.make_async_copy(folded.at[core, 0:block, :], pair_in, paired_sem.at[0])
-
-    def send_paired():
-        @pl.when(jnp.logical_not(fixed))
+        k = (xh + n_xh - (text // 2) % n_xh) % n_xh
+        return folded.at[core, pl.ds(pl.multiple_of((g * n_xh + k) * block, block), block), :]
+
+    def relay_copy(place):
+        return push(place, pair_in, paired_sem.at[2], paired_sem.at[0], half_peer)
+
+    def relay_paired():
+        @pl.when(near_other)
         def _():
-            pair_copy().start()
+            push(relay, relay, paired_sem.at[2], paired_sem.at[1], half_peer).wait_recv()
+            relay_copy(relay).start()
 
         @pl.when(fixed)
         def _():
-            pair_local().start()
+            relay_copy(held_place(r * cols + half_peer[1])).start()
 
     def unfold(g):
         def one(k, carry):
@@ -312,7 +363,7 @@
 
         lax.fori_loop(lo, hi, step, 0)
 
-    start, order = arrivals(n_y, 1.6)
+    start, order = arrivals(n_y, 1.55, 2.9)
     for piece in start:
         copy_of(piece).start()
 
@@ -355,6 +406,7 @@
                 missing[g].remove(piece)
                 if not missing[g]:
                     core_copy(g).start()
+                    pair_copies(g, lambda copy: copy.start())
                     flying.append((now + 3.0, g))
     land(1e9)
 
@@ -417,7 +469,6 @@
         return carry
 
     lax.fori_loop(0, n_wide, partial, 0)
-    send_paired()
 
     def wait_stats(d, carry):
         pltpu.make_async_remote_copy(
@@ -469,15 +520,18 @@
             z_copy(i, d).start()
         return carry
 
+    relay_paired()
     lax.fori_loop(0, n_wide, join, 0)
 
     @pl.when(jnp.logical_not(fixed))
     def _():
-        pair_copy().wait()
+        relay_copy(pair_in).wait_recv()
 
     @pl.when(fixed)
     def _():
-        pair_local().wait()
+        take = pltpu.make_async_copy(held_place(held_image), pair_in, paired_sem.at[3])
+        take.start()
+        take.wait()
 
     block_in = pair_in[...].astype(F32)
     paired[...] = jnp.concatenate([block_in[:own], block_in[own:]], axis=1)
@@ -506,6 +560,11 @@
             copy_of(piece).wait_send()
     for g in range(n_y):
         core_copy(g).wait_send()
+        pair_copies(g, lambda copy: copy.wait_send())
+
+    @pl.when(near_side)
+    def _():
+        relay_copy(relay).wait_send()
 
     def wait_stat_sends(d, carry):
         stat_copy(d).wait_send()
@@ -552,6 +611,7 @@
             vmem((n_img, width), BF16),
             vmem((own, width), BF16),
             vmem((2 * own, width // 2), BF16),
+            vmem((2 * own, width // 2), BF16),
             vmem((own, width), F32),
             vmem((2, n_text, width // 2), BF16),
             vmem((2, n_text, width // 2), BF16),
@@ -570,7 +630,8 @@
             vmem((n_wide, n_z, 2 * own, WIDE // 2), BF16),
             vmem((n_wide, n_z, 2 * own, WIDE // 2), BF16),
             dma((2,)),
-            dma((2,)),
+            dma((4,)),
+            dma((n_y, n_xh)),
             dma((1 + n_y, 4)),
             dma((1 + n_y, 4)),
             dma((2, n_y // 2, n_xh)),

time: 86.9 us -> 80.8 us (0.930)
  the two profiles are of different devices: /device:TPU:32 before, /device:TPU:1 now
where the time goes in v3:
time: 80.8 us; the launch traced here: 80.6 us
  Pallas kernels  76.6 us (95%)
  local copies, waits for them, and re-layouts  2.74 us (3%)
  between operations  1.28 us (2%)
    pallas_call x1, Pallas kernels, per_device(): pl.pallas_call(functools.partial(kernel, shape), out_shape=(jax.ShapeDtyp...  76.6 us
    unnamed x2, local copies, waits for them, and re-layouts  2.74 us

profile of v3, /device:TPU:1, one launch (start us, length us, event | category | flops | bytes accessed | tf_op | source)
XLA Modules:
  0.0 80.6 jit_solution(2256575225431043503)
XLA Ops:
  1.3 76.6 %shard_map.50 = (f32[1,24]{1,0:T(1,128)}, f32[24,1536]{1,0:T(8,128)}) custom-call(bf16[384,1536]{1,0:T(8,128)(2,1)} %images_hbm.1, bf16[24,1536]{1,0:T(8,128)(2,1)} %texts_hbm.1, f32[1]{0:T(128)S(6)} %copy.7.scale_ref), custom_call_target="tpu_custom_call" | custom-call | flops 3623878656 | bytes 1179648 | tf_op jit(solution)/shard_map/pallas_call | solution.py:595
  77.8 1.2 %copy.8 = f32[24]{0:T(128)} copy(f32[24]{0:T(128)} %bitcast.1) | data formatting | bytes 192
  79.0 1.6 %copy.9 = f32[24,1536]{1,0:T(8,128)} copy(f32[24,1536]{1,0:T(8,128)} %get-tuple-element.9) | data formatting | bytes 294912

commit v4 on v3

--- a/solution.py
+++ b/solution.py
@@ -523,6 +523,25 @@
     relay_paired()
     lax.fori_loop(0, n_wide, join, 0)
 
+    for piece in start:
+        copy_of(piece).wait_send()
+    for _, _, then in order:
+        for piece in then:
+            copy_of(piece).wait_send()
+    for g in range(n_y):
+        core_copy(g).wait_send()
+        pair_copies(g, lambda copy: copy.wait_send())
+
+    @pl.when(near_side)
+    def _():
+        relay_copy(relay).wait_send()
+
+    def wait_stat_sends(d, carry):
+        stat_copy(d).wait_send()
+        return carry
+
+    lax.fori_loop(1, cols, wait_stat_sends, 0)
+
     @pl.when(jnp.logical_not(fixed))
     def _():
         relay_copy(pair_in).wait_recv()
@@ -549,36 +568,12 @@
             value = value + jnp.concatenate([piece[:own], piece[own:]], axis=1)
         columns = pl.ds(pl.multiple_of(i * WIDE, WIDE), WIDE)
         grad_ref[:, columns] = value - paired[:, columns]
-        return carry
-
-    lax.fori_loop(0, n_wide, finish, 0)
-
-    for piece in start:
-        copy_of(piece).wait_send()
-    for _, _, then in order:
-        for piece in then:
-            copy_of(piece).wait_send()
-    for g in range(n_y):
-        core_copy(g).wait_send()
-        pair_copies(g, lambda copy: copy.wait_send())
-
-    @pl.when(near_side)
-    def _():
-        relay_copy(relay).wait_send()
-
-    def wait_stat_sends(d, carry):
-        stat_copy(d).wait_send()
-        return carry
-
-    lax.fori_loop(1, cols, wait_stat_sends, 0)
-
-    def wait_sends(i, carry):
         half_copy(i).wait_send()
         for d in range(1, n_z):
             z_copy(i, d).wait_send()
         return carry
 
-    lax.fori_loop(0, n_wide, wait_sends, 0)
+    lax.fori_loop(0, n_wide, finish, 0)
 
 
 def per_device(n_xh, n_xl, text_step, images, texts, logit_scale):

time: 80.8 us -> 79.4 us (0.983)
  Pallas kernels: 76.6 us -> 75.2 us
    pallas_call x1, Pallas kernels: 76.6 us -> 75.2 us  [per_device(): pl.pallas_call(functools.partial(kernel, shape), out_shape=(jax.ShapeDtyp...]
where the time goes in v4:
time: 79.4 us; the launch traced here: 79.2 us
  Pallas kernels  75.2 us (95%)
  local copies, waits for them, and re-layouts  2.74 us (3%)
  between operations  1.28 us (2%)
    pallas_call x1, Pallas kernels, per_device(): pl.pallas_call(functools.partial(kernel, shape), out_shape=(jax.ShapeDtyp...  75.2 us
    unnamed x2, local copies, waits for them, and re-layouts  2.74 us

profile of v4, /device:TPU:1, one launch (start us, length us, event | category | flops | bytes accessed | tf_op | source)
XLA Modules:
  0.0 79.2 jit_solution(11642998329058428666)
XLA Ops:
  1.3 75.2 %shard_map.50 = (f32[1,24]{1,0:T(1,128)}, f32[24,1536]{1,0:T(8,128)}) custom-call(bf16[384,1536]{1,0:T(8,128)(2,1)} %images_hbm.1, bf16[24,1536]{1,0:T(8,128)(2,1)} %texts_hbm.1, f32[1]{0:T(128)S(6)} %copy.7.scale_ref), custom_call_target="tpu_custom_call" | custom-call | flops 3623878656 | bytes 1179648 | tf_op jit(solution)/shard_map/pallas_call | solution.py:590
  76.4 1.2 %copy.8 = f32[24]{0:T(128)} copy(f32[24]{0:T(128)} %bitcast.1) | data formatting | bytes 192
  77.6 1.6 %copy.9 = f32[24,1536]{1,0:T(8,128)} copy(f32[24,1536]{1,0:T(8,128)} %get-tuple-element.9) | data formatting | bytes 294912

commit v5 on v4

--- a/solution.py
+++ b/solution.py
@@ -410,7 +410,7 @@
                     flying.append((now + 3.0, g))
     land(1e9)
 
-    chunk = 64 if n_img % 64 == 0 else n_img
+    chunk = 32 if n_img % 32 == 0 else n_img
 
     def soften(i, carry):
         part = pl.ds(pl.multiple_of(i * chunk, chunk), chunk)
@@ -514,7 +514,7 @@
         pair_sum[i] = own_part[i] * jnp.concatenate([me, me], axis=1) + x_in[i].astype(
             F32
         ) * jnp.concatenate([peer, peer], axis=1)
-        for d in range(1, n_z):
+        for d in sorted(range(1, n_z), key=lambda d: -min(d, n_z - d)):
             piece = pair_sum[i, pl.ds(pl.multiple_of(((z + d) % n_z) * own, 8), own), :]
             z_out[i, d] = jnp.concatenate([piece[:, :LANES], piece[:, LANES:]], axis=0).astype(BF16)
             z_copy(i, d).start()

time: 79.4 us -> 79.7 us (level)
  no operation moved by 1% of the time
where the time goes in v5:
time: 79.7 us; the launch traced here: 79.5 us
  Pallas kernels  75.5 us (95%)
  local copies, waits for them, and re-layouts  2.74 us (3%)
  between operations  1.28 us (2%)
    pallas_call x1, Pallas kernels, per_device(): pl.pallas_call(functools.partial(kernel, shape), out_shape=(jax.ShapeDtyp...  75.5 us
    unnamed x2, local copies, waits for them, and re-layouts  2.74 us

profile of v5, /device:TPU:1, one launch (start us, length us, event | category | flops | bytes accessed | tf_op | source)
XLA Modules:
  0.0 79.5 jit_solution(4800159286277211991)
XLA Ops:
  1.3 75.5 %shard_map.50 = (f32[1,24]{1,0:T(1,128)}, f32[24,1536]{1,0:T(8,128)}) custom-call(bf16[384,1536]{1,0:T(8,128)(2,1)} %images_hbm.1, bf16[24,1536]{1,0:T(8,128)(2,1)} %texts_hbm.1, f32[1]{0:T(128)S(6)} %copy.7.scale_ref), custom_call_target="tpu_custom_call" | custom-call | flops 3623878656 | bytes 1179648 | tf_op jit(solution)/shard_map/pallas_call | solution.py:590
  76.7 1.2 %copy.8 = f32[24]{0:T(128)} copy(f32[24]{0:T(128)} %bitcast.1) | data formatting | bytes 192
  77.9 1.6 %copy.9 = f32[24,1536]{1,0:T(8,128)} copy(f32[24,1536]{1,0:T(8,128)} %get-tuple-element.9) | data formatting | bytes 294912
